TPU v7x, 512 devices: a whole 4x8x8 slice. The times are simulated.
512 devices in a mesh: replica: 8 (over z_hi, core), fsdp: 64 (over z_lo, y, x).
Axes of the slice: x: 4, y: 8, z: 8 (z_hi: 4, z_lo: 2; z = z_hi * 2 + z_lo), core: 2. Of those that a mesh axis runs over, the one named last changes fastest.
Arguments:
- activations: bfloat16 [8, 8192, 4096], P('replica', 'fsdp'), may hold values from -6 to 6
- weight: bfloat16 [8, 4096, 512], P('replica', 'fsdp'), may hold values from -0.09375 to 0.09375
- cotangent: bfloat16 [8, 8192, 512], P('replica', 'fsdp'), may hold values from -6 to 6
- quantized: int32 [8, 1048576], P('replica', 'fsdp'), may hold values from -127 to 127
- scales: float32 [8, 4096], P('replica', 'fsdp'), may hold values from 0.004 to 0.04
- outer_params: float32 [1048576], P('fsdp'), may hold values from -6 to 6
- momentum: float32 [1048576], P('fsdp'), may hold values from -6 to 6
Outputs:
- projected: bfloat16 [8, 8192, 512], P('replica', 'fsdp')
- input_grad: bfloat16 [8, 8192, 4096], P('replica', 'fsdp')
- weight_grad: bfloat16 [8, 4096, 512], P('replica', 'fsdp')
- new_params: float32 [1048576], P('fsdp')
- new_momentum: float32 [1048576], P('fsdp')
Inputs may be any that keep to these rules, and one draw needn't show every extreme that they name: `quantized`: signed 8-bit codes.
All inputs are finite; a program needn't handle non-finite values.
Results may differ from a plain program's by a relative error of at most 0.008.
Values may be sent and summed in bfloat16 or wider, within the bound.
A program may use at most 64 MiB of HBM per device.

v0:
```python
import jax
import jax.numpy as jnp
from jax import lax
from jax.sharding import PartitionSpec as P

BLOCK = 256


def outer_update(delta, params_part, moment_part):
    moment_next = 0.9 * moment_part + delta
    params_next = params_part - 0.7 * (delta + 0.9 * moment_next)
    return (params_next, moment_next)


def body(activations, weight, cotangent, quantized, scales, outer_params, momentum):
    rows_local = activations[0]
    shard = weight[0]
    grad_rows = cotangent[0]
    feature_cols = lax.all_to_all(rows_local, "fsdp", split_axis=1, concat_axis=0, tiled=True)
    piece = lax.all_gather(shard, "fsdp", axis=0, tiled=True)
    cols = rows_local
    out_buf = jnp.dot(cols, piece, preferred_element_type=jnp.float32)
    part = lax.dot_general(
        grad_rows, piece, (((1,), (1,)), ((), ())), preferred_element_type=jnp.float32
    )
    input_grad = part.astype(jnp.bfloat16)
    cols = feature_cols
    gradient = lax.dot_general(
        cols,
        lax.all_gather(grad_rows, "fsdp", axis=0, tiled=True),
        (((0,), (0,)), ((), ())),
        preferred_element_type=jnp.float32,
    )
    projected = out_buf.astype(jnp.bfloat16)
    replicas = lax.axis_size("replica")
    codes = quantized[0].astype(jnp.float32).reshape(-1, BLOCK)
    local_term = (codes * scales[0][:, None]).reshape(-1)
    summed = lax.psum(local_term.astype(jnp.bfloat16), "replica").astype(jnp.float32)
    new_params, new_momentum = outer_update(summed / replicas, outer_params, momentum)
    return (
        projected[None],
        input_grad[None],
        gradient.astype(jnp.bfloat16)[None],
        new_params,
        new_momentum,
    )


def solution(mesh):
    placed = (
        P("replica", "fsdp", None),
        P("replica", "fsdp", None),
        P("replica", "fsdp", None),
        P("replica", "fsdp"),
        P("replica", "fsdp"),
        P("fsdp"),
        P("fsdp"),
    )
    return jax.shard_map(
        body,
        mesh=mesh,
        in_specs=placed,
        out_specs=(
            P("replica", "fsdp", None),
            P("replica", "fsdp", None),
            P("replica", "fsdp", None),
            P("fsdp"),
            P("fsdp"),
        ),
        check_vma=False,
    )
```

profile of v0, /device:TPU:2, one launch (start us, length us, event | category | flops | bytes accessed | tf_op | source)
XLA Modules:
  0.0 647.9 jit_solution(543613113976105079)
XLA Ops:
  7.2 0.0 copy-start
  7.2 0.0 copy-start.3
  7.2 0.0 copy-start.4
  7.2 0.0 copy-start.5
  7.2 0.0 copy-start.6
  7.2 0.0 all-gather.5.cloned.1.call-start
  7.3 0.7 all-gather.5.cloned.1.call-update
  8.0 0.0 all-gather.7.cloned.1.call-start
  8.0 0.7 all-gather.7.cloned.1.call-update
  8.7 2.3 copy.12
  11.0 12.6 %all-to-all-start = ((bf16[128,64,64]{0,2,1:T(8,128)(2,1)}), bf16[128,64,64]{0,2,1:T(8,128)(2,1)S(1)}, u32[]{:S(2)}, u32[]{:S(2)}) async-start(bf16[128,64,64]{0,2,1:T(8,128)(2,1)} %bitcast.5), calls=%async_computation | async-start | bytes 2097152 | tf_op jit(solution)/shard_map/all_to_all | solution.py:19
  23.6 0.0 copy-done
  23.6 0.1 broadcast_bitcast_fusion
  23.7 0.0 copy-done.4
  23.8 35.4 %psum.7 = bf16[16384]{0:T(1024)(128)(2,1)S(1)} all-reduce(bf16[16384]{0:T(1024)(128)(2,1)S(1)} %multiply_convert_fusion), channel_id=1, replica_groups=mesh['replica'=8,'fsdp'=64] {'replica'}, use_global_device_ids=true, to_apply=%region_0.0 | all-reduce | flops 16384 | bytes 65536 | tf_op jit(solution)/shard_map/psum | solution.py:38
  59.2 0.0 copy-done.6
  59.2 0.7 multiply_subtract_fusion
  59.9 262.2 %all-gather.5.cloned.1.call-done = bf16[1,4096,512]{2,1,0:T(8,128)(2,1)} async-done(((bf16[1,64,512]{2,1,0:T(8,128)(2,1)}), bf16[1,4096,512]{2,1,0:T(8,128)(2,1)}) %all-gather.5.cloned.1.call-update) | async-done | bytes 4194320 | tf_op jit(solution)/shard_map/all_gather | solution.py:20
  322.1 4.8 fusion.2
  326.9 0.0 copy-done.2
  326.9 1.4 fusion.9
  328.2 0.0 all-to-all-done
  328.2 307.3 %all-gather.7.cloned.1.call-done = bf16[1,8192,512]{2,1,0:T(8,128)(2,1)} async-done(((bf16[1,128,512]{2,1,0:T(8,128)(2,1)}), bf16[1,8192,512]{2,1,0:T(8,128)(2,1)}) %all-gather.7.cloned.1.call-update) | async-done | bytes 8388624 | tf_op jit(solution)/shard_map/all_gather | solution.py:30
  635.5 5.6 fusion.15
  (8 shorter events, 0.1 us)
Async XLA Ops:
  7.2 16.5 %copy-start = (f32[1,64]{1,0:T(1,128)S(1)}, f32[1,64]{1,0:T(1,128)}, u32[]{:S(2)}) copy-start(f32[1,64]{1,0:T(1,128)} %param.11) | copy-start | bytes 772
  7.2 314.9 %copy-start.3 = (bf16[1,128,512]{2,1,0:T(8,128)(2,1)S(1)}, bf16[1,128,512]{2,1,0:T(8,128)(2,1)}, u32[]{:S(2)}) copy-start(bf16[1,128,512]{2,1,0:T(8,128)(2,1)} %param.9) | copy-start | bytes 393220
  7.2 16.6 %copy-start.4 = (s32[1,16384]{1,0:T(1,128)S(1)}, s32[1,16384]{1,0:T(1,128)}, u32[]{:S(2)}) copy-start(s32[1,16384]{1,0:T(1,128)} %param.10) | copy-start | bytes 196612
  7.2 52.0 %copy-start.5 = (f32[16384]{0:T(1024)S(1)}, f32[16384]{0:T(1024)}, u32[]{:S(2)}) copy-start(f32[16384]{0:T(1024)} %param.12) | copy-start | bytes 196612
  7.2 52.0 %copy-start.6 = (f32[16384]{0:T(1024)S(1)}, f32[16384]{0:T(1024)}, u32[]{:S(2)}) copy-start(f32[16384]{0:T(1024)} %param.13) | copy-start | bytes 196612
  7.2 314.8 %all-gather.5.cloned.1.call-start = ((), (), s32[]{:S(2)}) async-start(), calls=%async_computation.1 | async-start | bytes 4259840 | tf_op jit(solution)/shard_map/all_gather | solution.py:20
  8.0 627.6 %all-gather.7.cloned.1.call-start = ((), (), s32[]{:S(2)}) async-start(), calls=%async_computation.2 | async-start | bytes 8519680 | tf_op jit(solution)/shard_map/all_gather | solution.py:30
  11.0 315.8 %copy-start.2 = (bf16[1,128,4096]{2,1,0:T(8,128)(2,1)S(1)}, bf16[1,128,4096]{2,1,0:T(8,128)(2,1)}, u32[]{:S(2)}) copy-start(bf16[1,128,4096]{2,1,0:T(8,128)(2,1)} %param.7) | copy-start | bytes 3145732
  11.0 317.2 %all-to-all-start = ((bf16[128,64,64]{0,2,1:T(8,128)(2,1)}), bf16[128,64,64]{0,2,1:T(8,128)(2,1)S(1)}, u32[]{:S(2)}, u32[]{:S(2)}) async-start(bf16[128,64,64]{0,2,1:T(8,128)(2,1)} %bitcast.5), calls=%async_computation | async-start | bytes 2097152 | tf_op jit(solution)/shard_map/all_to_all | solution.py:19
  322.1 4.8 copy-start.1
Sparse Core Ops, SparseCore 0:
  10.1 311.8 all-gather.4
  324.1 311.3 all-gather.6
where the time goes:
time: 648 us
  waiting for transfers between devices  571 us (88%)
  blocking collectives  35.4 us (5%)
  between operations  14.1 us (2%)
  starting transfers between devices  12.7 us (2%)
  matrix products  11.7 us (2%)
    all_gather x1, waiting for transfers between devices, body(): lax.all_gather(grad_rows, 'fsdp', axis=0, tiled=True)  307 us
    all_gather x1, waiting for transfers between devices, body(): piece = lax.all_gather(shard, 'fsdp', axis=0, tiled=True)  262 us
    psum x1, blocking collectives, body(): lax.psum(local_term.astype(jnp.bfloat16), 'replica').astype(jnp.float32)  35.4 us
  transfers between devices with their start and end apart: 3, of which 2 were waited for; matrix products, arithmetic and copies ran while one was open for 1% of the time, Pallas kernels for 0%

commit v1 on v0

v1 whole, which is shorter than its diff:
```python
import functools

import jax
import jax.numpy as jnp
from jax import lax
from jax.experimental import pallas as pl
from jax.experimental.pallas import tpu as pltpu
from jax.sharding import PartitionSpec as P

X, Y, Z, R = 4, 8, 2, 8
TOK, D, KV, SHARD = 128, 4096, 512, 64
HALF = D // Z
BLK = HALF // Y
HROWS = SHARD // 2
QROWS = HROWS // 2
SIDE = 128
PIECE = SIDE // R
MAXSEM = 256
ORDER = (4, 3, -3, 2, -2, 1, -1, 0)
BF, F32 = jnp.bfloat16, jnp.float32


def kernel(
    act, wsh, cot, quant, scale, par_in, mom_in,
    proj_out, ig_out, wg_out, par_out, mom_out,
    abuf, cbuf, wbuf, g0, g1, r0, x1, s1, r1, x0, da_own, da_far,
    p_send, p_recv, p_stage, wg_stage, term, r_rep, delta, qv, sv, pv, mv, pacc,
    send, recv, local,
):
    rep = lax.axis_index("replica")
    me = lax.axis_index("fsdp")
    z = lax.div(me, X * Y)
    y = lax.rem(lax.div(me, X), Y)
    x = lax.rem(me, X)
    far = 1 - z

    def at(zz, yy, xx):
        return (rep, zz * (X * Y) + yy * X + xx)

    def yk(k):
        return lax.rem(y + (k + Y), Y)

    def xk(j):
        return lax.rem(x + (j + X), X)

    z_dev = at(far, y, x)
    y_dev = {1: at(z, yk(1), x), -1: at(z, yk(-1), x)}
    x_dev = {j: at(z, y, xk(j)) for j in (1, 2, 3)}

    def r_dev(i):
        return (lax.rem(rep + i, R), me)

    ids = {}
    started = []

    def sem(key):
        return ids.setdefault(key, len(ids))

    def push(key, src, dst, dev):
        i = sem(key)
        copy = pltpu.make_async_remote_copy(
            src_ref=src, dst_ref=dst, send_sem=send.at[i], recv_sem=recv.at[i],
            device_id=dev, device_id_type=pl.DeviceIdType.MESH)
        copy.start()
        started.append(copy)

    def arrive(key, dst):
        i = sem(key)
        pltpu.make_async_remote_copy(
            src_ref=dst, dst_ref=dst, send_sem=send.at[i], recv_sem=recv.at[i],
            device_id=z_dev, device_id_type=pl.DeviceIdType.MESH).wait_recv()

    loads = {}

    def load(key, src, dst):
        copy = pltpu.make_async_copy(src, dst, local.at[len(loads)])
        copy.start()
        loads[key] = copy

    barrier = pltpu.get_barrier_semaphore()
    peers = [z_dev, y_dev[1], y_dev[-1]] + list(x_dev.values()) + [r_dev(i) for i in range(1, R)]
    for dev in peers:
        pl.semaphore_signal(barrier, inc=1, device_id=dev, device_id_type=pl.DeviceIdType.MESH)

    def cols(zz, k):
        return pl.ds(pl.multiple_of(zz * HALF + yk(k) * BLK, BLK), BLK)

    load("q", quant, qv)
    load("s", scale, sv)
    load("w", wsh.at[0], wbuf.at[y, x])
    load("c", cot.at[0], cbuf.at[pl.ds(0, TOK)])
    for k in ORDER:
        load(("a", k), act.at[0, :, cols(z, k)], abuf.at[yk(k), pl.ds(0, TOK)])
    load("p", par_in, pv)
    load("m", mom_in, mv)

    loads["q"].wait()
    loads["s"].wait()
    owner = lax.broadcasted_iota(jnp.int32, (SIDE, SHARD), 0) // 2
    lane = lax.broadcasted_iota(jnp.int32, (SIDE, SHARD), 1)
    row_scale = jnp.sum(jnp.where(owner == lane, sv[...], 0.0), axis=1, keepdims=True)
    term[...] = (qv[...].astype(F32) * row_scale).astype(BF)

    pl.semaphore_wait(barrier, len(peers))

    rows0 = pl.ds(0, HROWS)
    rows1 = pl.ds(HROWS, HROWS)
    quarter = {1: pl.ds(HROWS, QROWS), -1: pl.ds(HROWS + QROWS, QROWS)}
    half_of = {1: 0, -1: 1}

    def pair(h):
        return pl.ds(2 * h, 2)

    def send_a(k):
        push(("a", k), act.at[0, :, cols(far, k)], abuf.at[yk(k), pl.ds(TOK, TOK)], z_dev)

    def w1_first():
        for d in (1, -1):
            push(("w1y", d, 1), wsh.at[0, rows1], wbuf.at[y, x, rows1], y_dev[d])

    def w1_to_x(k, src):
        for j in (1, 3, 2):
            push(("w1x", k, j), src, wbuf.at[yk(k), x, rows1], x_dev[j])

    def w1_step(s):
        for d in (1, -1):
            k = -d * s
            if s < 4:
                ref = wbuf.at[yk(k), x, rows1]
                arrive(("w1y", d, s), ref)
                if s < 3:
                    push(("w1y", d, s + 1), ref, ref, y_dev[d])
                else:
                    part = wbuf.at[yk(k), x, quarter[d]]
                    push(("w1y", d, 4), part, part, y_dev[d])
            else:
                arrive(("w1y", d, 4), wbuf.at[yk(4), x, quarter[d]])
        for k in ((-s, s) if s < 4 else (4,)):
            w1_to_x(k, wbuf.at[yk(k), x, rows1])

    def w0_first():
        for j in (1, 3, 2):
            push(("w0x", j), wsh.at[0, rows0], wbuf.at[y, x, rows0], x_dev[j])

    def w0_row(k, h):
        return wbuf.at[yk(k), pair(h), rows0]

    def w0_x_arrived():
        for j in (1, 3, 2):
            arrive(("w0x", j), wbuf.at[y, xk(-j), rows0])
        loads["w"].wait()
        for h in (0, 1):
            for d in (1, -1):
                push(("w0y", d, 1, h), w0_row(0, h), w0_row(0, h), y_dev[d])

    def w0_step(s):
        for h in (0, 1):
            for d in (1, -1):
                k = -d * s
                if s < 4:
                    ref = w0_row(k, h)
                    arrive(("w0y", d, s, h), ref)
                    if s < 3 or half_of[d] == h:
                        push(("w0y", d, s + 1, h), ref, ref, y_dev[d])
                elif half_of[d] == h:
                    arrive(("w0y", d, 4, h), w0_row(4, h))

    def w1_x_arrived(k):
        for j in (1, 3, 2):
            arrive(("w1x", k, j), wbuf.at[yk(k), xk(-j), rows1])

    def input_grad(k):
        w = wbuf[yk(k)].reshape(BLK, KV)
        out = lax.dot_general(cbuf[...], w, (((1,), (1,)), ((), ())),
                              preferred_element_type=F32).astype(BF)
        da_far[yk(k)] = out[TOK:]
        push(("da", k), da_far.at[yk(k)], ig_out.at[0, :, cols(z, k)], z_dev)
        da_own[yk(k)] = out[:TOK]
        load(("da", k), da_own.at[yk(k)], ig_out.at[0, :, cols(z, k)])

    def weight_grad(k):
        loads["a", k].wait()
        arrive(("a", k), abuf.at[yk(k), pl.ds(TOK, TOK)])
        g = lax.dot_general(abuf[yk(k)], cbuf[...], (((0,), (0,)), ((), ())),
                            preferred_element_type=F32).astype(BF)
        g = g.reshape(X, SHARD, KV)
        g0[yk(k)] = g[:, :HROWS]
        g1[yk(k)] = g[:, HROWS:]

    def g0_send(s, d, h, k):
        ref = g0.at[yk(k), pair(h)]
        push(("g0y", d, s, h), ref, r0.at[half_of[d], s - 1, pair(h)], y_dev[d])

    def g0_first():
        for d in (1, -1):
            g0_send(1, d, half_of[d], 4)

    def g0_step(s):
        for d in (1, -1):
            k = d * (4 - s)
            for h in (0, 1):
                if s > 1 or half_of[d] == h:
                    slot = r0.at[half_of[d], s - 1, pair(h)]
                    arrive(("g0y", d, s, h), slot)
                    own = g0.at[yk(k), pair(h)]
                    own[...] = (own[...].astype(F32) + slot[...].astype(F32)).astype(BF)
                g0_send(s + 1, d, h, k)

    def g0_end():
        for d in (1, -1):
            for h in (0, 1):
                arrive(("g0y", d, 4, h), r0.at[half_of[d], 3, pair(h)])
        g0[y] = (g0[y].astype(F32) + r0[0, 3].astype(F32) + r0[1, 3].astype(F32)).astype(BF)
        for j in (1, 3, 2):
            push(("g0x", j), g0.at[y, xk(j)], x0.at[j - 1], x_dev[j])

    def g0_final():
        total = g0[y, x].astype(F32)
        for j in (1, 3, 2):
            arrive(("g0x", j), x0.at[j - 1])
            total += x0[j - 1].astype(F32)
        wg_stage[0:HROWS] = total.astype(BF)

    def g1_to_x(k):
        for j in (1, 3, 2):
            push(("g1x", k, j), g1.at[yk(k), xk(j)], x1.at[j - 1, yk(k)], x_dev[j])

    def g1_from_x(k):
        total = g1[yk(k), x].astype(F32)
        for j in (1, 3, 2):
            arrive(("g1x", k, j), x1.at[j - 1, yk(k)])
            total += x1[j - 1, yk(k)].astype(F32)
        return total

    g_quarter = {1: pl.ds(0, QROWS), -1: pl.ds(QROWS, QROWS)}

    def g1_first():
        s1[yk(4)] = g1_from_x(4).astype(BF)
        for d in (1, -1):
            push(("g1y", d, 1), s1.at[yk(4), g_quarter[d]], r1.at[half_of[d], 0, g_quarter[d]], y_dev[d])

    def g1_step(s):
        for d in (1, -1):
            k = d * (4 - s)
            total = g1_from_x(k)
            if s == 1:
                slot = r1.at[half_of[d], 0, g_quarter[d]]
                arrive(("g1y", d, 1), slot)
                got = slot[...].astype(F32)
                parts = [total[:QROWS], total[QROWS:]]
                parts[half_of[d]] += got
                s1[yk(k), 0:QROWS] = parts[0].astype(BF)
                s1[yk(k), QROWS:HROWS] = parts[1].astype(BF)
            else:
                slot = r1.at[half_of[d], s - 1]
                arrive(("g1y", d, s), slot)
                s1[yk(k)] = (total + slot[...].astype(F32)).astype(BF)
            push(("g1y", d, s + 1), s1.at[yk(k)], r1.at[half_of[d], s], y_dev[d])

    def g1_final():
        total = g1_from_x(0)
        for d in (1, -1):
            arrive(("g1y", d, 4), r1.at[half_of[d], 3])
            total += r1[half_of[d], 3].astype(F32)
        wg_stage[HROWS:SHARD] = total.astype(BF)

    mine = pl.ds(pl.multiple_of(rep * PIECE, PIECE), PIECE)

    def rep_first():
        for i in range(1, R):
            to = lax.rem(rep + i, R)
            push(("rs", i), term.at[pl.ds(pl.multiple_of(to * PIECE, PIECE), PIECE)], r_rep.at[i - 1], r_dev(i))

    def rep_sum():
        total = term[mine, :].astype(F32)
        for i in range(1, R):
            arrive(("rs", i), r_rep.at[i - 1])
            total += r_rep[i - 1].astype(F32)
        delta[mine, :] = total.astype(BF)
        for i in range(1, R):
            push(("ag", i), delta.at[mine], delta.at[mine], r_dev(i))

    def rep_final():
        for i in range(1, R):
            src = lax.rem(rep + (R - i), R)
            arrive(("ag", i), delta.at[pl.ds(pl.multiple_of(src * PIECE, PIECE), PIECE)])
        loads["p"].wait()
        loads["m"].wait()
        step = delta[...].astype(F32) * (1.0 / R)
        moment = 0.9 * mv[...] + step
        mv[...] = moment
        pv[...] = pv[...] - 0.7 * (step + 0.9 * moment)
        load("po", pv, par_out)
        load("mo", mv, mom_out)

    def project(ks, first):
        for n, k in enumerate(ks):
            part = jnp.dot(abuf[yk(k)], wbuf[yk(k)].reshape(BLK, KV), preferred_element_type=F32)
            if first and n == 0:
                pacc[...] = part
            else:
                pacc[...] += part

    push("c", cot.at[0], cbuf.at[pl.ds(TOK, TOK)], z_dev)
    w1_first()
    w0_first()
    send_a(4)
    w1_to_x(0, wsh.at[0, rows1])
    for k in ORDER[1:]:
        send_a(k)
    rep_first()

    w1_step(1)
    w0_x_arrived()
    w1_step(2)
    loads["c"].wait()
    arrive("c", cbuf.at[pl.ds(TOK, TOK)])
    weight_grad(4)
    g0_first()
    g1_to_x(4)
    w1_step(3)
    w0_step(1)
    w1_x_arrived(0)
    input_grad(0)
    weight_grad(3)
    weight_grad(-3)
    g0_step(1)
    g1_to_x(3)
    g1_to_x(-3)
    w1_step(4)
    w0_step(2)
    for k in (-1, 1):
        w1_x_arrived(k)
        input_grad(k)
    rep_sum()
    g1_first()
    weight_grad(2)
    weight_grad(-2)
    g0_step(2)
    g1_to_x(2)
    g1_to_x(-2)
    w0_step(3)
    for k in (-2, 2):
        w1_x_arrived(k)
        input_grad(k)
    g1_step(1)
    weight_grad(1)
    weight_grad(-1)
    g0_step(3)
    g1_to_x(1)
    g1_to_x(-1)
    for k in (-3, 3):
        w1_x_arrived(k)
        input_grad(k)
    weight_grad(0)
    g1_to_x(0)
    g1_step(2)
    w0_step(4)
    w1_x_arrived(4)
    input_grad(4)
    project(ORDER, True)
    p_send[...] = pacc[TOK:].astype(BF)
    push("p", p_send, p_recv, z_dev)
    g0_end()
    g1_step(3)
    rep_final()
    g0_final()
    g1_final()
    load("wo", wg_stage, wg_out.at[0])
    arrive("p", p_recv)
    p_stage[...] = (pacc[:TOK] + p_recv[...].astype(F32)).astype(BF)
    load("pr", p_stage, proj_out.at[0])
    for k in (0, -1, 1, -2, 2, -3, 3, 4):
        arrive(("da", k), ig_out.at[0, :, cols(far, k)])
    for copy in started:
        copy.wait_send()
    for k in ORDER:
        loads["da", k].wait()
    for key in ("po", "mo", "wo", "pr"):
        loads[key].wait()


def body(activations, weight, cotangent, quantized, scales, outer_params, momentum):
    any_spec = pl.BlockSpec(memory_space=pl.ANY)
    vm = pltpu.VMEM
    out = pl.pallas_call(
        kernel,
        out_shape=(
            jax.ShapeDtypeStruct((1, TOK, KV), BF),
            jax.ShapeDtypeStruct((1, TOK, D), BF),
            jax.ShapeDtypeStruct((1, SHARD, KV), BF),
            jax.ShapeDtypeStruct((SIDE, SIDE), F32),
            jax.ShapeDtypeStruct((SIDE, SIDE), F32),
        ),
        in_specs=[any_spec] * 7,
        out_specs=[any_spec] * 5,
        scratch_shapes=[
            vm((Y, 2 * TOK, BLK), BF),
            vm((2 * TOK, KV), BF),
            vm((Y, X, SHARD, KV), BF),
            vm((Y, X, HROWS, KV), BF),
            vm((Y, X, HROWS, KV), BF),
            vm((2, 4, X, HROWS, KV), BF),
            vm((3, Y, HROWS, KV), BF),
            vm((Y, HROWS, KV), BF),
            vm((2, 4, HROWS, KV), BF),
            vm((3, HROWS, KV), BF),
            vm((Y, TOK, BLK), BF),
            vm((Y, TOK, BLK), BF),
            vm((TOK, KV), BF),
            vm((TOK, KV), BF),
            vm((TOK, KV), BF),
            vm((SHARD, KV), BF),
            vm((SIDE, SIDE), BF),
            vm((R - 1, PIECE, SIDE), BF),
            vm((SIDE, SIDE), BF),
            vm((SIDE, SIDE), jnp.int32),
            vm((1, SHARD), F32),
            vm((SIDE, SIDE), F32),
            vm((SIDE, SIDE), F32),
            vm((2 * TOK, KV), F32),
            pltpu.SemaphoreType.DMA((MAXSEM,)),
            pltpu.SemaphoreType.DMA((MAXSEM,)),
            pltpu.SemaphoreType.DMA((32,)),
        ],
        compiler_params=pltpu.CompilerParams(
            collective_id=0, has_side_effects=True, vmem_limit_bytes=40 << 20),
        cost_estimate=pl.CostEstimate(
            flops=3 * 2 * TOK * D * KV, bytes_accessed=4 << 20, transcendentals=0),
    )(
        activations, weight, cotangent, quantized.reshape(SIDE, SIDE), scales,
        outer_params.reshape(SIDE, SIDE), momentum.reshape(SIDE, SIDE),
    )
    projected, input_grad, weight_grad, new_params, new_momentum = out
    return projected, input_grad, weight_grad, new_params.reshape(-1), new_momentum.reshape(-1)


def solution(mesh):
    placed = (
        P("replica", "fsdp", None),
        P("replica", "fsdp", None),
        P("replica", "fsdp", None),
        P("replica", "fsdp"),
        P("replica", "fsdp"),
        P("fsdp"),
        P("fsdp"),
    )
    return jax.shard_map(
        body,
        mesh=mesh,
        in_specs=placed,
        out_specs=(
            P("replica", "fsdp", None),
            P("replica", "fsdp", None),
            P("replica", "fsdp", None),
            P("fsdp"),
            P("fsdp"),
        ),
        check_vma=False,
    )
```

time: 648 us -> 62.5 us (0.10)
  the two profiles are of different devices: /device:TPU:2 before, /device:TPU:1 now
where the time goes in v1:
time: 62.5 us; the launch traced here: 62.2 us
  Pallas kernels  51.8 us (83%)
  local copies, waits for them, and re-layouts  9.66 us (15%)
  between operations  0.66 us (1%)
    pallas_call x1, Pallas kernels, body(): pl.pallas_call(kernel, out_shape=(jax.ShapeDtypeStruct((1, TOK, KV), BF),...  51.8 us
    unnamed x19, local copies, waits for them, and re-layouts  9.66 us

profile of v1, /device:TPU:1, one launch (start us, length us, event | category | flops | bytes accessed | tf_op | source)
XLA Modules:
  0.0 62.2 jit_solution(9494198063612126421)
XLA Ops:
  0.6 0.0 copy-start.6
  0.6 0.6 %copy-done.6 = f32[1,64]{1,0:T(1,128)S(1)} copy-done((f32[1,64]{1,0:T(1,128)S(1)}, f32[1,64]{1,0:T(1,128)}, u32[]{:S(2)}) %copy-start.6) | copy-done | bytes 280
  1.3 0.0 copy-start
  1.3 1.2 %copy-done = bf16[1,128,4096]{2,1,0:T(8,128)(2,1)S(1)} copy-done((bf16[1,128,4096]{2,1,0:T(8,128)(2,1)S(1)}, bf16[1,128,4096]{2,1,0:T(8,128)(2,1)}, u32[]{:S(2)}) %copy-start) | copy-done | bytes 1048600
  2.5 0.0 copy-start.1
  2.5 0.9 %copy-done.1 = bf16[1,128,512]{2,1,0:T(8,128)(2,1)S(1)} copy-done((bf16[1,128,512]{2,1,0:T(8,128)(2,1)S(1)}, bf16[1,128,512]{2,1,0:T(8,128)(2,1)}, u32[]{:S(2)}) %copy-start.1) | copy-done | bytes 131096
  3.4 0.0 copy-start.2
  3.4 0.8 %copy-done.2 = bf16[1,64,512]{2,1,0:T(8,128)(2,1)S(1)} copy-done((bf16[1,64,512]{2,1,0:T(8,128)(2,1)S(1)}, bf16[1,64,512]{2,1,0:T(8,128)(2,1)}, u32[]{:S(2)}) %copy-start.2) | copy-done | bytes 65560
  4.3 0.0 copy-start.3
  4.3 0.8 %copy-done.3 = s32[1,16384]{1,0:T(1,128)S(1)} copy-done((s32[1,16384]{1,0:T(1,128)S(1)}, s32[1,16384]{1,0:T(1,128)}, u32[]{:S(2)}) %copy-start.3) | copy-done | bytes 65560
  5.1 0.0 copy-start.4
  5.1 0.8 %copy-done.4 = f32[16384]{0:T(1024)S(1)} copy-done((f32[16384]{0:T(1024)S(1)}, f32[16384]{0:T(1024)}, u32[]{:S(2)}) %copy-start.4) | copy-done | bytes 65560
  5.9 0.0 copy-start.5
  5.9 0.8 %copy-done.5 = f32[16384]{0:T(1024)S(1)} copy-done((f32[16384]{0:T(1024)S(1)}, f32[16384]{0:T(1024)}, u32[]{:S(2)}) %copy-start.5) | copy-done | bytes 65560
  6.8 51.8 %shard_map.110 = (bf16[1,128,512]{2,1,0:T(8,128)(2,1)S(1)}, bf16[1,128,4096]{2,1,0:T(8,128)(2,1)S(1)}, bf16[1,64,512]{2,1,0:T(8,128)(2,1)S(1)}, f32[128,128]{1,0:T(8,128)S(1)}, f32[128,128]{1,0:T(8,128)S(1)}) custom-call(bf16[1,128,4096]{2,1,0:T(8,128)(2,1)S(1)} %copy-done, bf16[1,64,512]{2,1,0:T(8,128)(2,1)S(1)} %copy-done.2, ...), custom_call_target="tpu_custom_call" | custom-call | flops 1610612736 | bytes 4194304 | tf_op jit(solution)/shard_map/pallas_call | solution.py:386
  58.6 0.7 %copy.17 = bf16[1,128,512]{2,1,0:T(8,128)(2,1)} copy(bf16[1,128,512]{2,1,0:T(8,128)(2,1)S(1)} %get-tuple-element.20) | data formatting | bytes 262144
  59.3 1.0 %copy.18 = bf16[1,128,4096]{2,1,0:T(8,128)(2,1)} copy(bf16[1,128,4096]{2,1,0:T(8,128)(2,1)S(1)} %get-tuple-element.21) | data formatting | bytes 2097152
  60.3 0.6 %copy.19 = bf16[1,64,512]{2,1,0:T(8,128)(2,1)} copy(bf16[1,64,512]{2,1,0:T(8,128)(2,1)S(1)} %get-tuple-element.22) | data formatting | bytes 131072
  60.9 0.6 %copy.20 = f32[16384]{0:T(1024)} copy(f32[16384]{0:T(1024)S(1)} %bitcast.6) | data formatting | bytes 131072
  61.5 0.6 %copy.21 = f32[16384]{0:T(1024)} copy(f32[16384]{0:T(1024)S(1)} %bitcast.5) | data formatting | bytes 131072
Async XLA Ops:
  0.6 0.7 %copy-start.6 = (f32[1,64]{1,0:T(1,128)S(1)}, f32[1,64]{1,0:T(1,128)}, u32[]{:S(2)}) copy-start(f32[1,64]{1,0:T(1,128)} %scale.1) | copy-start | bytes 772
  1.3 1.2 %copy-start = (bf16[1,128,4096]{2,1,0:T(8,128)(2,1)S(1)}, bf16[1,128,4096]{2,1,0:T(8,128)(2,1)}, u32[]{:S(2)}) copy-start(bf16[1,128,4096]{2,1,0:T(8,128)(2,1)} %act.1) | copy-start | bytes 3145732
  2.5 0.9 %copy-start.1 = (bf16[1,128,512]{2,1,0:T(8,128)(2,1)S(1)}, bf16[1,128,512]{2,1,0:T(8,128)(2,1)}, u32[]{:S(2)}) copy-start(bf16[1,128,512]{2,1,0:T(8,128)(2,1)} %cot.1) | copy-start | bytes 393220
  3.4 0.8 %copy-start.2 = (bf16[1,64,512]{2,1,0:T(8,128)(2,1)S(1)}, bf16[1,64,512]{2,1,0:T(8,128)(2,1)}, u32[]{:S(2)}) copy-start(bf16[1,64,512]{2,1,0:T(8,128)(2,1)} %wsh.1) | copy-start | bytes 196612
  4.3 0.8 %copy-start.3 = (s32[1,16384]{1,0:T(1,128)S(1)}, s32[1,16384]{1,0:T(1,128)}, u32[]{:S(2)}) copy-start(s32[1,16384]{1,0:T(1,128)} %param.10) | copy-start | bytes 196612
  5.1 0.8 %copy-start.4 = (f32[16384]{0:T(1024)S(1)}, f32[16384]{0:T(1024)}, u32[]{:S(2)}) copy-start(f32[16384]{0:T(1024)} %param.12) | copy-start | bytes 196612
  5.9 0.8 %copy-start.5 = (f32[16384]{0:T(1024)S(1)}, f32[16384]{0:T(1024)}, u32[]{:S(2)}) copy-start(f32[16384]{0:T(1024)} %param.13) | copy-start | bytes 196612

commit v2 on v1

--- a/solution.py
+++ b/solution.py
@@ -15,7 +15,7 @@
 QROWS = HROWS // 2
 SIDE = 128
 PIECE = SIDE // R
-MAXSEM = 256
+NSEND, NRECV = 14, 80
 ORDER = (4, 3, -3, 2, -2, 1, -1, 0)
 BF, F32 = jnp.bfloat16, jnp.float32
 
@@ -25,7 +25,7 @@
     proj_out, ig_out, wg_out, par_out, mom_out,
     abuf, cbuf, wbuf, g0, g1, r0, x1, s1, r1, x0, da_own, da_far,
     p_send, p_recv, p_stage, wg_stage, term, r_rep, delta, qv, sv, pv, mv, pacc,
-    send, recv, local,
+    send, recv, local, ready,
 ):
     rep = lax.axis_index("replica")
     me = lax.axis_index("fsdp")
@@ -50,37 +50,47 @@
     def r_dev(i):
         return (lax.rem(rep + i, R), me)
 
-    ids = {}
-    started = []
-
-    def sem(key):
-        return ids.setdefault(key, len(ids))
+    send_ids, recv_ids = {}, {}
+
+    def together(key):
+        return key[:-1] if key[0] in ("w1x", "g1x", "w0x", "g0x", "rs", "ag", "da") else key
+
+    def remote(key, src, dst, dev):
+        i = send_ids.setdefault(key[0], len(send_ids))
+        j = recv_ids.setdefault(together(key), len(recv_ids))
+        assert i < NSEND and j < NRECV, (i, j)
+        return pltpu.make_async_remote_copy(
+            src_ref=src, dst_ref=dst, send_sem=send.at[i], recv_sem=recv.at[j],
+            device_id=dev, device_id_type=pl.DeviceIdType.MESH)
 
     def push(key, src, dst, dev):
-        i = sem(key)
-        copy = pltpu.make_async_remote_copy(
-            src_ref=src, dst_ref=dst, send_sem=send.at[i], recv_sem=recv.at[i],
-            device_id=dev, device_id_type=pl.DeviceIdType.MESH)
-        copy.start()
-        started.append(copy)
-
-    def arrive(key, dst):
-        i = sem(key)
+        remote(key, src, dst, dev).start()
+
+    def arrive(key, ref):
+        remote(key, ref, ref, z_dev).wait_recv()
+
+    def sent(kind, ref):
         pltpu.make_async_remote_copy(
-            src_ref=dst, dst_ref=dst, send_sem=send.at[i], recv_sem=recv.at[i],
-            device_id=z_dev, device_id_type=pl.DeviceIdType.MESH).wait_recv()
+            src_ref=ref, dst_ref=ref, send_sem=send.at[send_ids[kind]], recv_sem=recv.at[0],
+            device_id=z_dev, device_id_type=pl.DeviceIdType.MESH).wait_send()
 
     loads = {}
 
     def load(key, src, dst):
-        copy = pltpu.make_async_copy(src, dst, local.at[len(loads)])
-        copy.start()
-        loads[key] = copy
+        loads[key] = pltpu.make_async_copy(src, dst, local.at[len(loads)])
+        loads[key].start()
 
     barrier = pltpu.get_barrier_semaphore()
-    peers = [z_dev, y_dev[1], y_dev[-1]] + list(x_dev.values()) + [r_dev(i) for i in range(1, R)]
+    peers = [z_dev, y_dev[1], y_dev[-1]] + list(x_dev.values())
+
+    def greet(sem_ref, dev):
+        pl.semaphore_signal(sem_ref, inc=1, device_id=dev, device_id_type=pl.DeviceIdType.MESH)
+
     for dev in peers:
-        pl.semaphore_signal(barrier, inc=1, device_id=dev, device_id_type=pl.DeviceIdType.MESH)
+        greet(barrier, dev)
+
+    rank = rep
+    late = rank >= R // 2
 
     def cols(zz, k):
         return pl.ds(pl.multiple_of(zz * HALF + yk(k) * BLK, BLK), BLK)
@@ -94,14 +104,18 @@
     load("p", par_in, pv)
     load("m", mom_in, mv)
 
-    loads["q"].wait()
-    loads["s"].wait()
-    owner = lax.broadcasted_iota(jnp.int32, (SIDE, SHARD), 0) // 2
-    lane = lax.broadcasted_iota(jnp.int32, (SIDE, SHARD), 1)
-    row_scale = jnp.sum(jnp.where(owner == lane, sv[...], 0.0), axis=1, keepdims=True)
-    term[...] = (qv[...].astype(F32) * row_scale).astype(BF)
-
-    pl.semaphore_wait(barrier, len(peers))
+    pl.semaphore_wait(barrier, len(peers) + rank)
+    for i in range(1, R):
+        behind = lax.rem(rep + i, R) > rank
+
+        @pl.when(behind)
+        def _():
+            greet(barrier, r_dev(i))
+
+        @pl.when(jnp.logical_not(behind))
+        def _():
+            greet(ready, r_dev(i))
+
 
     rows0 = pl.ds(0, HROWS)
     rows1 = pl.ds(HROWS, HROWS)
@@ -146,8 +160,7 @@
         return wbuf.at[yk(k), pair(h), rows0]
 
     def w0_x_arrived():
-        for j in (1, 3, 2):
-            arrive(("w0x", j), wbuf.at[y, xk(-j), rows0])
+        arrive(("w0x", 0), x0)
         loads["w"].wait()
         for h in (0, 1):
             for d in (1, -1):
@@ -166,8 +179,7 @@
                     arrive(("w0y", d, 4, h), w0_row(4, h))
 
     def w1_x_arrived(k):
-        for j in (1, 3, 2):
-            arrive(("w1x", k, j), wbuf.at[yk(k), xk(-j), rows1])
+        arrive(("w1x", k, 0), x0)
 
     def input_grad(k):
         w = wbuf[yk(k)].reshape(BLK, KV)
@@ -176,7 +188,7 @@
         da_far[yk(k)] = out[TOK:]
         push(("da", k), da_far.at[yk(k)], ig_out.at[0, :, cols(z, k)], z_dev)
         da_own[yk(k)] = out[:TOK]
-        load(("da", k), da_own.at[yk(k)], ig_out.at[0, :, cols(z, k)])
+        pltpu.make_async_copy(da_own.at[yk(k)], ig_out.at[0, :, cols(z, k)], local.at[18]).start()
 
     def weight_grad(k):
         loads["a", k].wait()
@@ -216,8 +228,8 @@
 
     def g0_final():
         total = g0[y, x].astype(F32)
+        arrive(("g0x", 0), x0)
         for j in (1, 3, 2):
-            arrive(("g0x", j), x0.at[j - 1])
             total += x0[j - 1].astype(F32)
         wg_stage[0:HROWS] = total.astype(BF)
 
@@ -227,8 +239,8 @@
 
     def g1_from_x(k):
         total = g1[yk(k), x].astype(F32)
+        arrive(("g1x", k, 0), x0)
         for j in (1, 3, 2):
-            arrive(("g1x", k, j), x1.at[j - 1, yk(k)])
             total += x1[j - 1, yk(k)].astype(F32)
         return total
 
@@ -266,24 +278,34 @@
 
     mine = pl.ds(pl.multiple_of(rep * PIECE, PIECE), PIECE)
 
+    def dequantize():
+        loads["q"].wait()
+        loads["s"].wait()
+        owner = lax.broadcasted_iota(jnp.int32, (SIDE, SHARD), 0) // 2
+        lane = lax.broadcasted_iota(jnp.int32, (SIDE, SHARD), 1)
+        row_scale = jnp.sum(jnp.where(owner == lane, sv[...], 0.0), axis=1, keepdims=True)
+        term[...] = (qv[...].astype(F32) * row_scale).astype(BF)
+
     def rep_first():
+        @pl.when(rank < R - 1)
+        def _():
+            pl.semaphore_wait(ready, R - 1 - rank)
+
         for i in range(1, R):
             to = lax.rem(rep + i, R)
             push(("rs", i), term.at[pl.ds(pl.multiple_of(to * PIECE, PIECE), PIECE)], r_rep.at[i - 1], r_dev(i))
 
     def rep_sum():
         total = term[mine, :].astype(F32)
+        arrive(("rs", 0), r_rep)
         for i in range(1, R):
-            arrive(("rs", i), r_rep.at[i - 1])
             total += r_rep[i - 1].astype(F32)
         delta[mine, :] = total.astype(BF)
         for i in range(1, R):
             push(("ag", i), delta.at[mine], delta.at[mine], r_dev(i))
 
     def rep_final():
-        for i in range(1, R):
-            src = lax.rem(rep + (R - i), R)
-            arrive(("ag", i), delta.at[pl.ds(pl.multiple_of(src * PIECE, PIECE), PIECE)])
+        arrive(("ag", 0), r_rep)
         loads["p"].wait()
         loads["m"].wait()
         step = delta[...].astype(F32) * (1.0 / R)
@@ -301,57 +323,66 @@
             else:
                 pacc[...] += part
 
-    push("c", cot.at[0], cbuf.at[pl.ds(TOK, TOK)], z_dev)
+    push(("c",), cot.at[0], cbuf.at[pl.ds(TOK, TOK)], z_dev)
     w1_first()
     w0_first()
     send_a(4)
     w1_to_x(0, wsh.at[0, rows1])
-    for k in ORDER[1:]:
-        send_a(k)
-    rep_first()
-
+    dequantize()
     w1_step(1)
     w0_x_arrived()
     w1_step(2)
     loads["c"].wait()
-    arrive("c", cbuf.at[pl.ds(TOK, TOK)])
+    arrive(("c",), cbuf.at[pl.ds(TOK, TOK)])
+    send_a(3)
+    send_a(-3)
     weight_grad(4)
+    send_a(2)
     g0_first()
     g1_to_x(4)
     w1_step(3)
     w0_step(1)
     w1_x_arrived(0)
     input_grad(0)
+    pl.when(late)(rep_first)
     weight_grad(3)
+    send_a(-2)
     weight_grad(-3)
+    send_a(1)
     g0_step(1)
     g1_to_x(3)
     g1_to_x(-3)
     w1_step(4)
     w0_step(2)
-    for k in (-1, 1):
-        w1_x_arrived(k)
-        input_grad(k)
-    rep_sum()
+    w1_x_arrived(-1)
+    input_grad(-1)
+    w1_x_arrived(1)
+    input_grad(1)
     g1_first()
     weight_grad(2)
+    send_a(-1)
     weight_grad(-2)
+    send_a(0)
+    pl.when(jnp.logical_not(late))(rep_first)
     g0_step(2)
     g1_to_x(2)
     g1_to_x(-2)
     w0_step(3)
-    for k in (-2, 2):
-        w1_x_arrived(k)
-        input_grad(k)
+    w1_x_arrived(-2)
+    input_grad(-2)
+    w1_x_arrived(2)
+    input_grad(2)
+    pl.when(late)(rep_sum)
     g1_step(1)
     weight_grad(1)
     weight_grad(-1)
     g0_step(3)
     g1_to_x(1)
     g1_to_x(-1)
-    for k in (-3, 3):
-        w1_x_arrived(k)
-        input_grad(k)
+    w1_x_arrived(-3)
+    input_grad(-3)
+    w1_x_arrived(3)
+    input_grad(3)
     weight_grad(0)
     g1_to_x(0)
     g1_step(2)
@@ -360,24 +391,45 @@
     input_grad(4)
     project(ORDER, True)
     p_send[...] = pacc[TOK:].astype(BF)
-    push("p", p_send, p_recv, z_dev)
+    push(("p",), p_send, p_recv, z_dev)
+    pl.when(jnp.logical_not(late))(rep_sum)
     g0_end()
     g1_step(3)
     rep_final()
     g0_final()
     g1_final()
     load("wo", wg_stage, wg_out.at[0])
-    arrive("p", p_recv)
+    arrive(("p",), p_recv)
     p_stage[...] = (pacc[:TOK] + p_recv[...].astype(F32)).astype(BF)
     load("pr", p_stage, proj_out.at[0])
-    for k in (0, -1, 1, -2, 2, -3, 3, 4):
-        arrive(("da", k), ig_out.at[0, :, cols(far, k)])
-    for copy in started:
-        copy.wait_send()
-    for k in ORDER:
-        loads["da", k].wait()
+    arrive(("da", 0), da_far)
+    steps = wbuf.at[pl.ds(0, 7), pl.ds(0, 2)]
+    small = s1.at[pl.ds(0, 7)]
+    for kind, ref in (
+        ("c", p_recv), ("p", p_recv), ("a", da_far), ("da", da_far), ("w0x", x0), ("g0x", x0), ("w1x", x1), ("g1x", x1),
+        ("w0y", steps), ("g0y", steps), ("w1y", small), ("g1y", small), ("rs", r_rep), ("ag", r_rep),
+    ):
+        sent(kind, ref)
+    pltpu.make_async_copy(da_own, da_far, local.at[18]).wait()
     for key in ("po", "mo", "wo", "pr"):
         loads[key].wait()
+
+
+def write_out(*refs):
+    ins, outs, stages = refs[:5], refs[5:10], refs[10:15]
+    in_sem, out_sem = refs[15:]
+    step = TOK // 4
+    parts = [(1, (0, pl.ds(i * step, step))) for i in range(4)] + [(n, (0,)) for n in (0, 2)]
+    parts += [(n, (slice(None),)) for n in (3, 4)]
+    there = [pltpu.make_async_copy(ins[n].at[p], stages[n].at[p], in_sem.at[i]) for i, (n, p) in enumerate(parts)]
+    back = [pltpu.make_async_copy(stages[n].at[p], outs[n].at[p], out_sem.at[i]) for i, (n, p) in enumerate(parts)]
+    for copy in there:
+        copy.start()
+    for first, second in zip(there, back):
+        first.wait()
+        second.start()
+    for copy in back:
+        copy.wait()
 
 
 def body(activations, weight, cotangent, quantized, scales, outer_params, momentum):
@@ -419,19 +471,28 @@
             vm((SIDE, SIDE), F32),
             vm((SIDE, SIDE), F32),
             vm((2 * TOK, KV), F32),
-            pltpu.SemaphoreType.DMA((MAXSEM,)),
-            pltpu.SemaphoreType.DMA((MAXSEM,)),
-            pltpu.SemaphoreType.DMA((32,)),
+            pltpu.SemaphoreType.DMA((NSEND,)),
+            pltpu.SemaphoreType.DMA((NRECV,)),
+            pltpu.SemaphoreType.DMA((19,)),
+            pltpu.SemaphoreType.REGULAR,
         ],
         compiler_params=pltpu.CompilerParams(
-            collective_id=0, has_side_effects=True, vmem_limit_bytes=40 << 20),
+            collective_id=0, has_side_effects=True, vmem_limit_bytes=60 << 20),
         cost_estimate=pl.CostEstimate(
             flops=3 * 2 * TOK * D * KV, bytes_accessed=4 << 20, transcendentals=0),
     )(
         activations, weight, cotangent, quantized.reshape(SIDE, SIDE), scales,
         outer_params.reshape(SIDE, SIDE), momentum.reshape(SIDE, SIDE),
     )
-    projected, input_grad, weight_grad, new_params, new_momentum = out
+    projected, input_grad, weight_grad, new_params, new_momentum = pl.pallas_call(
+        write_out,
+        out_shape=tuple(jax.ShapeDtypeStruct(a.shape, a.dtype) for a in out),
+        in_specs=[any_spec] * 5,
+        out_specs=[any_spec] * 5,
+        scratch_shapes=[vm(a.shape, a.dtype) for a in out]
+        + [pltpu.SemaphoreType.DMA((8,)), pltpu.SemaphoreType.DMA((8,))],
+        compiler_params=pltpu.CompilerParams(vmem_limit_bytes=60 << 20),
+    )(*out)
     return projected, input_grad, weight_grad, new_params.reshape(-1), new_momentum.reshape(-1)
 
 

time: 62.5 us -> 49.2 us (0.79)
  local copies, waits for them, and re-layouts: 9.66 us -> 0 us
  Pallas kernels: 51.8 us -> 48.4 us
    unnamed x19 -> x0, local copies, waits for them, and re-layouts: 9.66 us -> none
    pallas_call x1, Pallas kernels: 51.8 us -> 46.2 us  [body(): pl.pallas_call(kernel, out_shape=(jax.ShapeDtypeStruct((1, TOK, KV), BF),...]
    pallas_call x0 -> x1, Pallas kernels: none -> 2.15 us  [body(): pl.pallas_call(write_out, out_shape=tuple((jax.ShapeDtypeStruct(a.shape,...]
where the time goes in v2:
time: 49.2 us; the launch traced here: 49 us
  Pallas kernels  48.4 us (98%)
  between operations  0.64 us (1%)
    pallas_call x1, Pallas kernels, body(): pl.pallas_call(kernel, out_shape=(jax.ShapeDtypeStruct((1, TOK, KV), BF),...  46.2 us
    pallas_call x1, Pallas kernels, body(): pl.pallas_call(write_out, out_shape=tuple((jax.ShapeDtypeStruct(a.shape,...  2.15 us

profile of v2, /device:TPU:1, one launch (start us, length us, event | category | flops | bytes accessed | tf_op | source)
XLA Modules:
  0.0 49.0 jit_solution(127518556958222415)
XLA Ops:
  0.6 46.2 %shard_map.110 = (bf16[1,128,512]{2,1,0:T(8,128)(2,1)}, bf16[1,128,4096]{2,1,0:T(8,128)(2,1)}, bf16[1,64,512]{2,1,0:T(8,128)(2,1)}, f32[128,128]{1,0:T(8,128)}, f32[128,128]{1,0:T(8,128)}) custom-call(bf16[1,128,4096]{2,1,0:T(8,128)(2,1)} %act.1, bf16[1,64,512]{2,1,0:T(8,128)(2,1)} %wsh.1, bf16[1,128,512]{2,1,0:T(8,128)(2,1)} %cot.1, s32[128,128]{1,0:T(8,128)} %bitcast.5, ...), custom_call_target="tpu_custom_call" | custom-call | flops 1610612736 | bytes 4194304 | tf_op jit(solution)/shard_map/pallas_call | solution.py:438
  46.9 2.2 %shard_map.111 = (bf16[1,128,512]{2,1,0:T(8,128)(2,1)}, bf16[1,128,4096]{2,1,0:T(8,128)(2,1)}, bf16[1,64,512]{2,1,0:T(8,128)(2,1)}, f32[128,128]{1,0:T(8,128)}, f32[128,128]{1,0:T(8,128)}) custom-call(bf16[1,128,512]{2,1,0:T(8,128)(2,1)} %get-tuple-element.15.refs_0_, bf16[1,128,4096]{2,1,0:T(8,128)(2,1)} %get-tuple-element.16.refs_1_, ...), custom_call_target="tpu_custom_call" | custom-call | tf_op jit(solution)/shard_map/pallas_call | solution.py:487

commit v3 on v2

--- a/solution.py
+++ b/solution.py
@@ -86,11 +86,13 @@
     def greet(sem_ref, dev):
         pl.semaphore_signal(sem_ref, inc=1, device_id=dev, device_id_type=pl.DeviceIdType.MESH)
 
+    peers.append((rep + 1 - 2 * lax.rem(rep, 2), me))
     for dev in peers:
         greet(barrier, dev)
 
-    rank = rep
-    late = rank >= R // 2
+    slab = lax.div(rep, 2)
+    slabs = R // 2
+    late = slab >= slabs // 2
 
     def cols(zz, k):
         return pl.ds(pl.multiple_of(zz * HALF + yk(k) * BLK, BLK), BLK)
@@ -104,18 +106,21 @@
     load("p", par_in, pv)
     load("m", mom_in, mv)
 
-    pl.semaphore_wait(barrier, len(peers) + rank)
-    for i in range(1, R):
-        behind = lax.rem(rep + i, R) > rank
-
-        @pl.when(behind)
-        def _():
-            greet(barrier, r_dev(i))
-
-        @pl.when(jnp.logical_not(behind))
-        def _():
-            greet(ready, r_dev(i))
-
+    pl.semaphore_wait(barrier, len(peers) + 2 * slab)
+
+    def greet_slabs():
+        for step in range(1, slabs):
+            other = lax.rem(slab + step, slabs)
+
+            @pl.when(other > slab)
+            def _():
+                for c in (0, 1):
+                    greet(barrier, (other * 2 + c, me))
+
+            @pl.when(other < slab)
+            def _():
+                for c in (0, 1):
+                    greet(ready, (other * 2 + c, me))
 
     rows0 = pl.ds(0, HROWS)
     rows1 = pl.ds(HROWS, HROWS)
@@ -287,9 +292,9 @@
         term[...] = (qv[...].astype(F32) * row_scale).astype(BF)
 
     def rep_first():
-        @pl.when(rank < R - 1)
+        @pl.when(slab < slabs - 1)
         def _():
-            pl.semaphore_wait(ready, R - 1 - rank)
+            pl.semaphore_wait(ready, 2 * (slabs - 1 - slab))
 
         for i in range(1, R):
             to = lax.rem(rep + i, R)
@@ -316,18 +321,17 @@
         load("mo", mv, mom_out)
 
     def project(ks, first):
-        for n, k in enumerate(ks):
-            part = jnp.dot(abuf[yk(k)], wbuf[yk(k)].reshape(BLK, KV), preferred_element_type=F32)
-            if first and n == 0:
-                pacc[...] = part
-            else:
-                pacc[...] += part
+        rows = jnp.concatenate([abuf[yk(k)] for k in ks], axis=1)
+        matrix = jnp.concatenate([wbuf[yk(k)].reshape(BLK, KV) for k in ks], axis=0)
+        part = jnp.dot(rows, matrix, preferred_element_type=F32)
+        pacc[...] = part if first else pacc[...] + part
 
     push(("c",), cot.at[0], cbuf.at[pl.ds(TOK, TOK)], z_dev)
     w1_first()
     w0_first()
     send_a(4)
     w1_to_x(0, wsh.at[0, rows1])
+    greet_slabs()
     dequantize()
     w1_step(1)
     w0_x_arrived()
@@ -367,12 +371,12 @@
     g0_step(2)
     g1_to_x(2)
     g1_to_x(-2)
+    pl.when(late)(rep_sum)
     w0_step(3)
     w1_x_arrived(-2)
     input_grad(-2)
     w1_x_arrived(2)
     input_grad(2)
-    pl.when(late)(rep_sum)
     g1_step(1)
     weight_grad(1)
     weight_grad(-1)
@@ -386,12 +390,13 @@
     weight_grad(0)
     g1_to_x(0)
     g1_step(2)
+    project((0, 1, -1, 2, -2), True)
     w0_step(4)
     w1_x_arrived(4)
-    input_grad(4)
-    project(ORDER, True)
+    project((3, -3, 4), False)
     p_send[...] = pacc[TOK:].astype(BF)
     push(("p",), p_send, p_recv, z_dev)
+    input_grad(4)
     pl.when(jnp.logical_not(late))(rep_sum)
     g0_end()
     g1_step(3)

time: 49.2 us -> 47.1 us (0.957); the launches traced: 49 us -> 46.4 us
  Pallas kernels: 48.4 us -> 45.7 us
    pallas_call x1, Pallas kernels: 46.2 us -> 43.6 us  [body(): pl.pallas_call(kernel, out_shape=(jax.ShapeDtypeStruct((1, TOK, KV), BF),...]
where the time goes in v3:
time: 47.1 us; the launch traced here: 46.4 us
  Pallas kernels  45.7 us (97%)
  between operations  0.64 us (1%)
    pallas_call x1, Pallas kernels, body(): pl.pallas_call(kernel, out_shape=(jax.ShapeDtypeStruct((1, TOK, KV), BF),...  43.6 us
    pallas_call x1, Pallas kernels, body(): pl.pallas_call(write_out, out_shape=tuple((jax.ShapeDtypeStruct(a.shape,...  2.15 us

profile of v3, /device:TPU:1, one launch (start us, length us, event | category | flops | bytes accessed | tf_op | source)
XLA Modules:
  0.0 46.4 jit_solution(7703935319408553073)
XLA Ops:
  0.6 43.6 %shard_map.110 = (bf16[1,128,512]{2,1,0:T(8,128)(2,1)}, bf16[1,128,4096]{2,1,0:T(8,128)(2,1)}, bf16[1,64,512]{2,1,0:T(8,128)(2,1)}, f32[128,128]{1,0:T(8,128)}, f32[128,128]{1,0:T(8,128)}) custom-call(bf16[1,128,4096]{2,1,0:T(8,128)(2,1)} %act.1, bf16[1,64,512]{2,1,0:T(8,128)(2,1)} %wsh.1, bf16[1,128,512]{2,1,0:T(8,128)(2,1)} %cot.1, s32[128,128]{1,0:T(8,128)} %bitcast.5, ...), custom_call_target="tpu_custom_call" | custom-call | flops 1610612736 | bytes 4194304 | tf_op jit(solution)/shard_map/pallas_call | solution.py:443
  44.2 2.2 %shard_map.111 = (bf16[1,128,512]{2,1,0:T(8,128)(2,1)}, bf16[1,128,4096]{2,1,0:T(8,128)(2,1)}, bf16[1,64,512]{2,1,0:T(8,128)(2,1)}, f32[128,128]{1,0:T(8,128)}, f32[128,128]{1,0:T(8,128)}) custom-call(bf16[1,128,512]{2,1,0:T(8,128)(2,1)} %get-tuple-element.15.refs_0_, bf16[1,128,4096]{2,1,0:T(8,128)(2,1)} %get-tuple-element.16.refs_1_, ...), custom_call_target="tpu_custom_call" | custom-call | tf_op jit(solution)/shard_map/pallas_call | solution.py:492

commit v4 on v3

--- a/solution.py
+++ b/solution.py
@@ -102,7 +102,7 @@
     load("w", wsh.at[0], wbuf.at[y, x])
     load("c", cot.at[0], cbuf.at[pl.ds(0, TOK)])
     for k in ORDER:
-        load(("a", k), act.at[0, :, cols(z, k)], abuf.at[yk(k), pl.ds(0, TOK)])
+        pltpu.make_async_copy(act.at[0, :, cols(z, k)], abuf.at[yk(k), pl.ds(0, TOK)], local.at[10]).start()
     load("p", par_in, pv)
     load("m", mom_in, mv)
 
@@ -193,10 +193,11 @@
         da_far[yk(k)] = out[TOK:]
         push(("da", k), da_far.at[yk(k)], ig_out.at[0, :, cols(z, k)], z_dev)
         da_own[yk(k)] = out[:TOK]
-        pltpu.make_async_copy(da_own.at[yk(k)], ig_out.at[0, :, cols(z, k)], local.at[18]).start()
+        pltpu.make_async_copy(da_own.at[yk(k)], ig_out.at[0, :, cols(z, k)], local.at[11]).start()
 
     def weight_grad(k):
-        loads["a", k].wait()
+        if k == ORDER[0]:
+            pltpu.make_async_copy(da_own, da_far, local.at[10]).wait()
         arrive(("a", k), abuf.at[yk(k), pl.ds(TOK, TOK)])
         g = lax.dot_general(abuf[yk(k)], cbuf[...], (((0,), (0,)), ((), ())),
                             preferred_element_type=F32).astype(BF)
@@ -415,7 +416,7 @@
         ("w0y", steps), ("g0y", steps), ("w1y", small), ("g1y", small), ("rs", r_rep), ("ag", r_rep),
     ):
         sent(kind, ref)
-    pltpu.make_async_copy(da_own, da_far, local.at[18]).wait()
+    pltpu.make_async_copy(da_own, da_far, local.at[11]).wait()
     for key in ("po", "mo", "wo", "pr"):
         loads[key].wait()
 
@@ -423,8 +424,8 @@
 def write_out(*refs):
     ins, outs, stages = refs[:5], refs[5:10], refs[10:15]
     in_sem, out_sem = refs[15:]
-    step = TOK // 4
-    parts = [(1, (0, pl.ds(i * step, step))) for i in range(4)] + [(n, (0,)) for n in (0, 2)]
+    step = TOK // 8
+    parts = [(1, (0, pl.ds(i * step, step))) for i in range(8)] + [(n, (0,)) for n in (0, 2)]
     parts += [(n, (slice(None),)) for n in (3, 4)]
     there = [pltpu.make_async_copy(ins[n].at[p], stages[n].at[p], in_sem.at[i]) for i, (n, p) in enumerate(parts)]
     back = [pltpu.make_async_copy(stages[n].at[p], outs[n].at[p], out_sem.at[i]) for i, (n, p) in enumerate(parts)]
@@ -478,7 +479,7 @@
             vm((2 * TOK, KV), F32),
             pltpu.SemaphoreType.DMA((NSEND,)),
             pltpu.SemaphoreType.DMA((NRECV,)),
-            pltpu.SemaphoreType.DMA((19,)),
+            pltpu.SemaphoreType.DMA((12,)),
             pltpu.SemaphoreType.REGULAR,
         ],
         compiler_params=pltpu.CompilerParams(
@@ -495,7 +496,7 @@
         in_specs=[any_spec] * 5,
         out_specs=[any_spec] * 5,
         scratch_shapes=[vm(a.shape, a.dtype) for a in out]
-        + [pltpu.SemaphoreType.DMA((8,)), pltpu.SemaphoreType.DMA((8,))],
+        + [pltpu.SemaphoreType.DMA((12,)), pltpu.SemaphoreType.DMA((12,))],
         compiler_params=pltpu.CompilerParams(vmem_limit_bytes=60 << 20),
     )(*out)
     return projected, input_grad, weight_grad, new_params.reshape(-1), new_momentum.reshape(-1)

time: 47.1 us -> 47.1 us (level)
  no operation moved by 1% of the time
where the time goes in v4:
time: 47.1 us; the launch traced here: 46.4 us
  Pallas kernels  45.8 us (97%)
  between operations  0.64 us (1%)
    pallas_call x1, Pallas kernels, body(): pl.pallas_call(kernel, out_shape=(jax.ShapeDtypeStruct((1, TOK, KV), BF),...  43.5 us
    pallas_call x1, Pallas kernels, body(): pl.pallas_call(write_out, out_shape=tuple((jax.ShapeDtypeStruct(a.shape,...  2.26 us

profile of v4, /device:TPU:1, one launch (start us, length us, event | category | flops | bytes accessed | tf_op | source)
XLA Modules:
  0.0 46.4 jit_solution(18114613574437322960)
XLA Ops:
  0.6 43.5 %shard_map.110 = (bf16[1,128,512]{2,1,0:T(8,128)(2,1)}, bf16[1,128,4096]{2,1,0:T(8,128)(2,1)}, bf16[1,64,512]{2,1,0:T(8,128)(2,1)}, f32[128,128]{1,0:T(8,128)}, f32[128,128]{1,0:T(8,128)}) custom-call(bf16[1,128,4096]{2,1,0:T(8,128)(2,1)} %act.1, bf16[1,64,512]{2,1,0:T(8,128)(2,1)} %wsh.1, bf16[1,128,512]{2,1,0:T(8,128)(2,1)} %cot.1, s32[128,128]{1,0:T(8,128)} %bitcast.5, ...), custom_call_target="tpu_custom_call" | custom-call | flops 1610612736 | bytes 4194304 | tf_op jit(solution)/shard_map/pallas_call | solution.py:444
  44.2 2.3 %shard_map.111 = (bf16[1,128,512]{2,1,0:T(8,128)(2,1)}, bf16[1,128,4096]{2,1,0:T(8,128)(2,1)}, bf16[1,64,512]{2,1,0:T(8,128)(2,1)}, f32[128,128]{1,0:T(8,128)}, f32[128,128]{1,0:T(8,128)}) custom-call(bf16[1,128,512]{2,1,0:T(8,128)(2,1)} %get-tuple-element.15.refs_0_, bf16[1,128,4096]{2,1,0:T(8,128)(2,1)} %get-tuple-element.16.refs_1_, ...), custom_call_target="tpu_custom_call" | custom-call | tf_op jit(solution)/shard_map/pallas_call | solution.py:493
